TPU v7x, 32 devices: a whole 2x2x4 slice. The times are simulated.
32 devices in a mesh: parts: 2 (over y), grp: 4 (over z), band: 2 (over x), half: 2 (over core).
Axes of the slice: x: 2, y: 2, z: 4, core: 2. Of those that a mesh axis runs over, the one named last changes fastest.
Arguments:
- pair_list: int32 [64, 2], P(('parts', 'grp', 'half')), parts along dimension 0, may hold values from 0 to 127, as said below
- kernel: bfloat16 [64, 1024, 1024], P(('parts', 'grp', 'half')), parts along dimension 0, may hold values from 7.785857e-07 to 0.0078125
- facet_areas: float32 [256, 1024], P(('parts', 'grp')), parts along dimension 0, may hold values from 0.5 to 2
- heat_load: float32 [256, 1024], P(('parts', 'grp')), parts along dimension 0, may hold values from 0.2 to 2
- start_t4: float32 [256, 1024], P(('parts', 'grp')), parts along dimension 0, may hold values from 0.5 to 2
- material: int32 [256, 1024], P(('parts', 'grp')), parts along dimension 0, may hold values from 0 to 7
- coating: int32 [256], P(('parts', 'grp')), parts along dimension 0, may hold values from 0 to 3
- emis_table: float32 [4, 8], replicated, may hold values from 0.2 to 0.9
- share_table: float32 [8, 8], replicated, may hold values from 0.05 to 0.3
Outputs:
- radiosity: bfloat16 [256, 8, 1024], P(('parts', 'grp'), 'band'), parts along dimension 0
- temperature: float32 [256, 1024], P(('parts', 'grp')), parts along dimension 0
There are 2 independent parts, one for each index of `parts`. A program takes and returns all parts, laid end to end along the dimension named above; an argument that names none is the same for every part. Nothing has to cross between parts.
Inputs may be any that keep to these rules, and one draw needn't show every extreme that they name: `pair_list`: each row holds two group numbers, the first below the second.
All inputs are finite; a program needn't handle non-finite values.
Results may differ from a plain program's by a relative error of at most 0.0017.
Values may be sent and summed in bfloat16 or wider, within the bound.
A program may use at most 64 MiB of HBM per device.

v0:
```python
import functools

import jax
import jax.numpy as jnp
from jax import lax
from jax.experimental import pallas as pl
from jax.experimental.pallas import tpu as pltpu
from jax.sharding import PartitionSpec as P

SWEEPS = 2
F32 = jnp.float32
BF16 = jnp.bfloat16


def exchange(kernel_dims, *refs):
    Z, X, C, S, ppd, NB, NM, NCLS = kernel_dims
    (
        pair_ref, coat_ref, emis_ref, share_ref,
        mat_hbm, start_hbm, areas_hbm, heat_hbm, kern_hbm, inc_ref,
        held, mats, kern, info, rows_out, rows_in, rad, gath, last,
        held_sem, mat_sem, kern_sem, info_send, info_recv, row_send, row_recv, send_sem, recv_sem,
    ) = refs
    z, x, c = lax.axis_index("grp"), lax.axis_index("band"), lax.axis_index("half")
    groups_dev, FG = mats.shape
    MESH = pl.DeviceIdType.MESH

    loads = [
        pltpu.make_async_copy(source, held.at[a], held_sem.at[a])
        for a, source in enumerate((start_hbm, areas_hbm, heat_hbm))
    ]
    loads.insert(0, pltpu.make_async_copy(mat_hbm, mats, mat_sem))
    for load in loads:
        load.start()
    load_kern = pltpu.make_async_copy(kern_hbm.at[pl.ds(x * ppd, ppd)], kern, kern_sem)
    load_kern.start()

    barrier = pltpu.get_barrier_semaphore()
    z_peers = [lax.rem(z + k, Z) for k in range(1, Z)]
    x_peers = [lax.rem(x + k, X) for k in range(1, X)]
    c_peers = [lax.rem(c + k, C) for k in range(1, C)]
    z_devices = [{"grp": t} for t in z_peers]
    c_devices = [{"half": t} for t in c_peers]
    far_devices = [{"grp": t, "half": u} for t in z_peers for u in c_peers]
    everyone = z_devices + c_devices + far_devices + [{"band": t} for t in x_peers]
    for peer in everyone:
        pl.semaphore_signal(barrier, inc=1, device_id=peer, device_id_type=MESH)

    width = X * S * NB
    per_tile = 128 // width
    mine_info = z * C + c
    lane = lax.broadcasted_iota(jnp.int32, (8, 128), 1)
    row = lax.broadcasted_iota(jnp.int32, (8, 128), 0)
    first_lane = lax.rem(mine_info, per_tile) * width
    slot_at = lane // NB - first_lane // NB
    keys = jnp.zeros((8, 128), jnp.int32)
    for xx in range(X):
        for s in range(S):
            group = pair_ref[xx * ppd + s % ppd, s // ppd]
            keys = jnp.where(slot_at == xx * S + s, group * NB + lane % NB, keys)
    columns = jnp.full((8, 128), -1, jnp.int32)
    band_of = lax.broadcasted_iota(jnp.int32, (S * NB, 128), 0)
    own_key = jnp.zeros((S * NB, 128), jnp.int32)
    for s in range(S):
        group = jnp.int32(0)
        for xx in range(X):
            group = jnp.where(x == xx, pair_ref[xx * ppd + s % ppd, s // ppd], group)
        columns = jnp.where(row == s, group, columns)
        own_key = jnp.where(band_of // NB == s, group * NB + band_of % NB, own_key)
    info[mine_info] = jnp.where(row == 7, keys, columns)

    pl.semaphore_wait(barrier, len(everyone))

    def info_copy(n, block, peer):
        return pltpu.make_async_remote_copy(
            src_ref=info.at[block],
            dst_ref=info.at[block],
            send_sem=info_send.at[n],
            recv_sem=info_recv.at[block],
            device_id=peer,
            device_id_type=MESH,
        )

    info_copies = []
    for n, peer in enumerate(z_devices + c_devices + far_devices):
        copy = info_copy(n, mine_info, peer)
        copy.start()
        info_copies.append(copy)
    coat = jnp.zeros((groups_dev, 1), jnp.int32)
    group_row = lax.broadcasted_iota(jnp.int32, (groups_dev, 1), 0)
    for g in range(groups_dev):
        coat = jnp.where(group_row == g, coat_ref[g], coat)
    for load in loads:
        load.wait()
    combined = (coat * NM + mats[...]).astype(F32)
    for t in z_peers:
        info_copy(0, t * C + c, everyone[0]).wait_recv()

    want = jnp.concatenate([info[t * C + c] for t in range(Z)], axis=0)[:, :groups_dev]
    local = lax.broadcasted_iota(jnp.int32, (Z * 8, groups_dev), 1) + z * groups_dev
    pick = jnp.where(want == local, jnp.ones(want.shape, F32), 0.0)
    row_copies = []
    for half in range(2):
        for a in range(2):
            source = combined if half + a == 0 else held[half * 2 + a - 1]
            found = jnp.dot(
                pick, source, precision=lax.Precision.HIGHEST, preferred_element_type=F32
            )
            for t in range(Z):
                rows_out[half, t, a * S : (a + 1) * S, :] = found[t * 8 : t * 8 + S, :]
        for k in range(1, Z):
            copy = pltpu.make_async_remote_copy(
                src_ref=rows_out.at[half, z_peers[k - 1]],
                dst_ref=rows_in.at[half, k - 1],
                send_sem=row_send.at[half, k - 1],
                recv_sem=row_recv.at[half, k - 1],
                device_id=z_devices[k - 1],
                device_id_type=MESH,
            )
            copy.start()
            row_copies.append(copy)

    def arrived(half):
        rows = rows_out[half, z]
        for k in range(1, Z):
            row_copies[half * (Z - 1) + k - 1].wait_recv()
            rows = rows + rows_in[half, k - 1]
        return rows

    band_col = lax.broadcasted_iota(jnp.int32, (NB, 1), 0)

    def table_column(ref, m):
        column = jnp.zeros((NB, 1), F32)
        for b in range(NB):
            column = jnp.where(band_col == b, ref[m, b], column)
        return column

    share_cols = [table_column(share_ref, m) for m in range(NM)]
    emis_cols = [table_column(emis_ref, k) for k in range(NCLS)]
    rows = arrived(0)
    weights, emis_slots, emit_sums = [], [], []
    for s in range(S):
        ids = rows[s : s + 1, :]
        emis = jnp.broadcast_to(emis_cols[0], (NB, FG))
        material = ids
        for k in range(1, NCLS):
            emis = jnp.where(ids > k * NM - 0.5, emis_cols[k], emis)
            material = jnp.where(ids > k * NM - 0.5, ids - k * NM, material)
        share = jnp.broadcast_to(share_cols[0], (NB, FG))
        for m in range(1, NM):
            share = jnp.where(material > m - 0.5, share_cols[m], share)
        weight = emis * share
        weights.append(weight)
        emis_slots.append(emis)
        emit_sums.append(jnp.sum(weight, axis=0, keepdims=True))
        rad[s] = (weight * rows[S + s : S + s + 1, :]).astype(BF16)
    load_kern.wait()

    def block_of(zz, xx, cc):
        return (zz * C + cc) * X + xx

    rows_block = S * NB
    for sweep in range(SWEEPS):
        mine = block_of(z, x, c)
        started = []
        final = sweep == SWEEPS - 1
        buffer = last if final else gath.at[sweep]

        def send(block, peer):
            copy = pltpu.make_async_remote_copy(
                src_ref=buffer.at[block],
                dst_ref=buffer.at[block],
                send_sem=send_sem.at[sweep, len(started)],
                recv_sem=recv_sem.at[sweep, block],
                device_id=peer,
                device_id_type=pl.DeviceIdType.MESH,
            )
            copy.start()
            started.append(copy)

        def receive(block):
            pltpu.make_async_remote_copy(
                src_ref=buffer.at[block],
                dst_ref=buffer.at[block],
                send_sem=send_sem.at[sweep, 0],
                recv_sem=recv_sem.at[sweep, block],
                device_id=everyone[0],
                device_id_type=pl.DeviceIdType.MESH,
            ).wait_recv()

        to_first, to_second = [], []
        for q in range(ppd):
            to_first.append(
                lax.dot_general(
                    rad[ppd + q], kern[q], (((1,), (1,)), ((), ())), preferred_element_type=F32
                )
            )
            to_second.append(jnp.dot(rad[q], kern[q], preferred_element_type=F32))
        buffer[mine] = jnp.concatenate(to_first + to_second, axis=0).astype(buffer.dtype)

        for t in z_peers:
            send(mine, {"grp": t})
        for t in x_peers:
            send(mine, {"band": t})
        for t in c_peers:
            send(mine, {"half": t})
        for xt in x_peers:
            block = block_of(z, xt, c)
            receive(block)
            for t in c_peers:
                send(block, {"half": t})
        for zt in z_peers:
            block = block_of(zt, x, c)
            receive(block)
            for t in x_peers:
                send(block, {"band": t})
            for t in c_peers:
                send(block, {"half": t})
        for zt in z_peers:
            for xt in x_peers:
                block = block_of(zt, xt, c)
                receive(block)
                for t in c_peers:
                    send(block, {"half": t})
        for ct in c_peers:
            for zt in [z] + z_peers:
                for xt in [x] + x_peers:
                    receive(block_of(zt, xt, ct))

        if sweep == 0:
            for t in z_peers + [z]:
                for u in c_peers:
                    info_copy(0, t * C + u, everyone[0]).wait_recv()
            tiles = []
            for t in range(Z * C // per_tile):
                tile = info[t * per_tile]
                for n in range(1, per_tile):
                    tile = tile + info[t * per_tile + n]
                tiles.append(tile[7:8, :])
            key_row = jnp.concatenate(tiles, axis=1)
            area_rows = arrived(1)

        terms = buffer[...].reshape(-1, FG)
        count = terms.shape[0]
        if not final:
            select = jnp.where(own_key[:, :1] == key_row, jnp.ones((rows_block, count), F32), 0.0)
            incoming = jnp.dot(select.astype(BF16), terms, preferred_element_type=F32)
            for s in range(S):
                emis = emis_slots[s]
                irradiance = incoming[s * NB : (s + 1) * NB, :] / area_rows[s : s + 1, :]
                absorbed = jnp.sum(emis * irradiance, axis=0, keepdims=True)
                fourth = (absorbed + area_rows[S + s : S + s + 1, :]) / emit_sums[s]
                rad[s] = (weights[s] * fourth + (1.0 - emis) * irradiance).astype(BF16)
        else:
            row_key = lax.broadcasted_iota(jnp.int32, (groups_dev * NB, count), 0) + z * (groups_dev * NB)
            select = jnp.where(row_key == key_row, jnp.ones(row_key.shape, F32), 0.0).astype(BF16)
            high = terms.astype(BF16)
            low = (terms - high.astype(F32)).astype(BF16)
            inc_ref[...] = jnp.dot(select, high, preferred_element_type=F32) + jnp.dot(
                select, low, preferred_element_type=F32
            )
        for copy in started:
            copy.wait_send()
    for copy in info_copies + row_copies:
        copy.wait_send()


def on_device(
    pair_list, kernel, facet_areas, heat_load, start_t4, material, coating, emis_table, share_table
):
    groups_dev, FG = facet_areas.shape
    NCLS, NB = emis_table.shape
    NM = share_table.shape[0]
    Z, X, C = lax.axis_size("grp"), lax.axis_size("band"), lax.axis_size("half")
    x = lax.axis_index("band")
    pairs_dev = pair_list.shape[0]
    ppd = pairs_dev // X
    S = 2 * ppd
    D = Z * X * C
    bands_dev = NB // X

    def emis_of(classes):
        result = jnp.zeros((classes.shape[0], NB), F32)
        for k in range(NCLS):
            result = jnp.where((classes == k)[:, None], emis_table[k][None, :], result)
        return result

    smem = pl.BlockSpec(memory_space=pltpu.SMEM)
    dma = pltpu.SemaphoreType.DMA
    incoming = pl.pallas_call(
        functools.partial(exchange, (Z, X, C, S, ppd, NB, NM, NCLS)),
        out_shape=jax.ShapeDtypeStruct((groups_dev * NB, FG), F32),
        in_specs=[smem] * 4 + [pl.BlockSpec(memory_space=pl.ANY)] * 5,
        out_specs=pl.BlockSpec(memory_space=pltpu.VMEM),
        scratch_shapes=[
            pltpu.VMEM((3, groups_dev, FG), F32),
            pltpu.VMEM((groups_dev, FG), jnp.int32),
            pltpu.VMEM((ppd, FG, FG), BF16),
            pltpu.VMEM((Z * C, 8, 128), jnp.int32),
            pltpu.VMEM((2, Z, 2 * S, FG), F32),
            pltpu.VMEM((2, Z - 1, 2 * S, FG), F32),
            pltpu.VMEM((S, NB, FG), BF16),
            pltpu.VMEM((SWEEPS - 1, D, S * NB, FG), BF16),
            pltpu.VMEM((D, S * NB, FG), F32),
            dma((3,)),
            dma(()),
            dma(()),
            dma((Z * C,)),
            dma((Z * C,)),
            dma((2, Z - 1)),
            dma((2, Z - 1)),
            dma((SWEEPS, D)),
            dma((SWEEPS, D)),
        ],
        compiler_params=pltpu.CompilerParams(
            collective_id=0, has_side_effects=True, vmem_limit_bytes=48 * 1024 * 1024
        ),
        cost_estimate=pl.CostEstimate(flops=200_000_000, bytes_accessed=8_000_000, transcendentals=0),
    )(
        pair_list, coating, emis_table, share_table,
        material, start_t4, facet_areas, heat_load, kernel,
    )

    emis = emis_of(coating)[:, :, None]
    share = jnp.zeros((groups_dev, NB, FG), F32)
    for m in range(NM):
        share = jnp.where((material == m)[:, None, :], share_table[m][None, :, None], share)
    weight = emis * share
    emit_sum = jnp.sum(weight, axis=1)
    irradiance = incoming.reshape(groups_dev, NB, FG) / facet_areas[:, None, :]
    absorbed = jnp.sum(emis * irradiance, axis=1)
    fourth = (absorbed + heat_load) / emit_sum

    def mine(rows):
        return lax.dynamic_slice_in_dim(rows, x * bands_dev, bands_dev, 1)

    share_mine = jnp.zeros((groups_dev, bands_dev, FG), F32)
    table = mine(share_table)
    for m in range(NM):
        share_mine = jnp.where((material == m)[:, None, :], table[m][None, :, None], share_mine)
    emis_mine = mine(emis)
    incoming_mine = mine(incoming.reshape(groups_dev, NB, FG))
    radiosity = emis_mine * share_mine * fourth[:, None, :] + (1.0 - emis_mine) * (
        incoming_mine / facet_areas[:, None, :]
    )
    return (radiosity.astype(BF16), fourth**0.25)


def solution(mesh):
    return jax.shard_map(
        on_device,
        mesh=mesh,
        in_specs=(
            P(("parts", "grp", "half"), None),
            P(("parts", "grp", "half"), None, None),
            P(("parts", "grp"), None),
            P(("parts", "grp"), None),
            P(("parts", "grp"), None),
            P(("parts", "grp"), None),
            P(("parts", "grp")),
            P(),
            P(),
        ),
        out_specs=(P(("parts", "grp"), "band", None), P(("parts", "grp"), None)),
        check_vma=False,
    )
```

profile of v0, /device:TPU:9, one launch (start us, length us, event | category | flops | bytes accessed | tf_op | source)
XLA Modules:
  0.0 71.1 jit_solution(2997502206030191182)
XLA Ops:
  0.6 0.8 %copy.11.refs_0_ = s32[4,2]{1,0:T(4,128)S(1)} copy(s32[4,2]{0,1:T(2,128)} %param.9) | data formatting | bytes 64 | tf_op args[0]
  1.4 0.7 broadcast_compare_fusion.11
  2.1 0.8 %slice_bitcast_fusion.19 = (f32[8]{0:T(128)S(1)}, f32[8]{0:T(128)S(1)}, f32[8]{0:T(128)S(1)}, f32[8]{0:T(128)S(1)}) fusion(f32[4,8]{1,0:T(4,128)} %refs_2_.1), kind=kLoop, calls=%fused_computation.36 | loop fusion | bytes 256 | tf_op jit(solution)/shard_map/jit(_where)/broadcast_in_dim | solution.py:284
  2.9 0.8 %constant_dynamic-slice_fusion = f32[8,4]{1,0:T(8,128)S(1)} fusion(f32[8,8]{1,0:T(8,128)} %refs_3_.1, s32[]{:T(128)S(6)} %select_n.88), kind=kLoop, calls=%fused_computation.15 | loop fusion | bytes 260 | tf_op jit(solution)/shard_map/dynamic_slice | solution.py:334
  3.7 1.0 %slice_bitcast_fusion.7 = (f32[8]{0:T(128)S(1)}, f32[8]{0:T(128)S(1)}, f32[8]{0:T(128)S(1)}, f32[8]{0:T(128)S(1)}, f32[8]{0:T(128)S(1)}, /*index=5*/f32[8]{0:T(128)S(1)}, f32[8]{0:T(128)S(1)}, f32[8]{0:T(128)S(1)}) fusion(f32[8,8]{1,0:T(8,128)} %refs_3_.1), kind=kLoop, calls=%fused_computation.24 | loop fusion | bytes 512 | tf_op jit(solution)/shard_map/jit(_where)/broadcast_in_dim | solution.py:326
  4.6 0.1 select_select_fusion
  4.7 0.1 broadcast_subtract_fusion
  4.8 1.1 %broadcast_compare_fusion.7 = (pred[32,1024]{1,0:T(8,128)(4,1)S(1)}, pred[32,1024]{1,0:T(8,128)(4,1)S(1)}, pred[32,1024]{1,0:T(8,128)(4,1)S(1)}, pred[32,1024]{1...) fusion(s32[32,1024]{1,0:T(8,128)} %refs_4_.1), kind=kLoop, calls=%fused_computation.12 | loop fusion | flops 262144 | bytes 393216 | tf_op jit(solution)/shard_map/eq | solution.py:339
  5.9 0.0 copy-start
  5.9 0.9 %copy-done = f32[32,1024]{1,0:T(8,128)S(1)} copy-done((f32[32,1024]{1,0:T(8,128)S(1)}, f32[32,1024]{1,0:T(8,128)}, u32[]{:S(2)}) %copy-start) | copy-done | bytes 131096
  6.8 0.0 copy-start.1
  6.8 0.9 %copy-done.1 = s32[32,1024]{1,0:T(8,128)S(1)} copy-done((s32[32,1024]{1,0:T(8,128)S(1)}, s32[32,1024]{1,0:T(8,128)}, u32[]{:S(2)}) %copy-start.1) | copy-done | bytes 131096
  7.7 0.0 copy-start.2
  7.7 0.9 %copy-done.2 = f32[32,1024]{1,0:T(8,128)S(1)} copy-done((f32[32,1024]{1,0:T(8,128)S(1)}, f32[32,1024]{1,0:T(8,128)}, u32[]{:S(2)}) %copy-start.2) | copy-done | bytes 131096
  8.6 0.0 copy-start.3
  8.6 0.9 %copy-done.3 = f32[32,1024]{1,0:T(8,128)S(1)} copy-done((f32[32,1024]{1,0:T(8,128)S(1)}, f32[32,1024]{1,0:T(8,128)}, u32[]{:S(2)}) %copy-start.3) | copy-done | bytes 131096
  9.5 0.0 copy-start.4
  9.5 0.7 copy-done.4
  10.2 0.0 copy-start.5
  10.2 0.7 copy-done.5
  10.9 0.0 copy-start.6
  10.9 0.7 copy-done.6
  11.5 55.2 %shard_map.104 = f32[256,1024]{1,0:T(8,128)S(1)} custom-call(s32[4,2]{1,0:T(4,128)S(1)} %copy.11.refs_0_, s32[32]{0:T(128)S(1)} %copy-done.6, f32[4,8]{1,0:T(4,128)S(1)} %copy-done.5, f32[8,8]{1,0:T(8,128)S(1)} %copy-done.4, s32[32,1024]{1,0:T(8,128)S(1)} %copy-done.1, f32[32,1024]{1,0:T(8,128)S(1)} %copy-done.3, f32[32,1024]{1,0:T(8,128)S(1)} %copy-done, ...), custom_call_target="tpu_custom_call" | custom-call | flops 200000000 | bytes 8000000 | tf_op jit(solution)/shard_map/pallas_call | solution.py:289
  66.7 1.6 %multiply_reduce_fusion.1 = (f32[32,1024]{1,0:T(8,128)S(1)}, f32[32,1024]{1,0:T(8,128)S(1)}) fusion(f32[32,1024]{1,0:T(8,128)S(1)} %copy-done, f32[32,8]{1,0:T(8,128)S(1)} %select_select_fusion, f32[256,1024]{1,0:T(8,128)S(1)} %shard_map.104, f32[8]{0:T(128)S(1)} %get-tuple-element.30, pred[32,1024]{1,0:T(8,128)(4,1)S(1)} %get-tuple-element.15, ...), kind=kLoop, calls=%fused_computation.1 | loop fusion | flops 3342336 | bytes 1705216 | tf_op jit(solution)/shard_map/reduce_sum | solution.py:330
  68.4 0.7 %broadcast_power_fusion = (f32[32,1024]{1,0:T(8,128)}, f32[32,1024]{1,0:T(8,128)S(1)}) fusion(f32[32,1024]{1,0:T(8,128)S(1)} %get-tuple-element.3, f32[32,1024]{1,0:T(8,128)S(1)} %get-tuple-element.2, f32[32,1024]{1,0:T(8,128)S(1)} %copy-done.2), kind=kLoop, calls=%fused_computation.4 | loop fusion | flops 65536 | bytes 655360 | tf_op jit(solution)/shard_map/pow | solution.py:345
  69.1 2.0 %add_convert_fusion = bf16[32,4,1024]{2,1,0:T(4,128)(2,1)} fusion(f32[32,8,1024]{2,1,0:T(8,128)S(1)} %bitcast.42, s32[]{:T(128)S(6)} %select_n.88, f32[32,1024]{1,0:T(8,128)S(1)} %copy-done, f32[32,4]{1,0:T(8,128)S(1)} %get-tuple-element.6, f32[32,1024]{1,0:T(8,128)S(1)} %get-tuple-element.5, f32[4]{0:T(128)S(1)} %get-tuple-element.17, ...), kind=kLoop, calls=%fused_computation.2 | loop fusion | flops 1835008 | bytes 1311876 | tf_op jit(solution)/shard_map/convert_element_type | solution.py:345
  (1 shorter events, 0.0 us)
Async XLA Ops:
  5.9 0.9 %copy-start = (f32[32,1024]{1,0:T(8,128)S(1)}, f32[32,1024]{1,0:T(8,128)}, u32[]{:S(2)}) copy-start(f32[32,1024]{1,0:T(8,128)} %refs_6_.1) | copy-start | bytes 393220
  6.8 0.9 %copy-start.1 = (s32[32,1024]{1,0:T(8,128)S(1)}, s32[32,1024]{1,0:T(8,128)}, u32[]{:S(2)}) copy-start(s32[32,1024]{1,0:T(8,128)} %refs_4_.1) | copy-start | bytes 393220
  7.7 0.9 %copy-start.2 = (f32[32,1024]{1,0:T(8,128)S(1)}, f32[32,1024]{1,0:T(8,128)}, u32[]{:S(2)}) copy-start(f32[32,1024]{1,0:T(8,128)} %refs_7_.1) | copy-start | bytes 393220
  8.6 0.9 %copy-start.3 = (f32[32,1024]{1,0:T(8,128)S(1)}, f32[32,1024]{1,0:T(8,128)}, u32[]{:S(2)}) copy-start(f32[32,1024]{1,0:T(8,128)} %refs_5_.1) | copy-start | bytes 393220
  9.5 0.7 copy-start.4
  10.2 0.7 copy-start.5
  10.9 0.7 copy-start.6
where the time goes:
time: 71.6 us; the launch traced here: 71.1 us
  Pallas kernels  55.2 us (77%)
  local copies, waits for them, and re-layouts  8.98 us (13%)
  other arithmetic  6.22 us (9%)
    pallas_call x1, Pallas kernels, on_device(): pl.pallas_call(functools.partial(exchange, (Z, X, C, S, ppd, NB, NM, NCLS...  55.2 us
    unnamed x15, local copies, waits for them, and re-layouts  6.4 us
    convert_element_type x1, other arithmetic, on_device(): return (radiosity.astype(BF16), fourth ** 0.25)  2.01 us
    reduce_sum x1, other arithmetic, on_device(): absorbed = jnp.sum(emis * irradiance, axis=1)  1.61 us

commit v1 on v0

--- a/solution.py
+++ b/solution.py
@@ -14,11 +14,13 @@
 
 def exchange(kernel_dims, *refs):
     Z, X, C, S, ppd, NB, NM, NCLS = kernel_dims
+    slots, BD = X * S, NB // X
     (
         pair_ref, coat_ref, emis_ref, share_ref,
-        mat_hbm, start_hbm, areas_hbm, heat_hbm, kern_hbm, inc_ref,
-        held, mats, kern, info, rows_out, rows_in, rad, gath, last,
-        held_sem, mat_sem, kern_sem, info_send, info_recv, row_send, row_recv, send_sem, recv_sem,
+        mat_hbm, start_hbm, areas_hbm, heat_hbm, kern_hbm, inc_ref, absorbed_ref,
+        held, mats, kern, info, rows_out, rows_in, rows_all, rad, stage, gath, last, sum_first, sum_last,
+        held_sem, mat_sem, kern_sem, info_send, info_recv, row_send, row_recv,
+        all_send, all_recv, sum_send, sum_recv, send_sem, recv_sem,
     ) = refs
     z, x, c = lax.axis_index("grp"), lax.axis_index("band"), lax.axis_index("half")
     groups_dev, FG = mats.shape
@@ -31,7 +33,7 @@
     loads.insert(0, pltpu.make_async_copy(mat_hbm, mats, mat_sem))
     for load in loads:
         load.start()
-    load_kern = pltpu.make_async_copy(kern_hbm.at[pl.ds(x * ppd, ppd)], kern, kern_sem)
+    load_kern = pltpu.make_async_copy(kern_hbm, kern, kern_sem)
     load_kern.start()
 
     barrier = pltpu.get_barrier_semaphore()
@@ -39,33 +41,35 @@
     x_peers = [lax.rem(x + k, X) for k in range(1, X)]
     c_peers = [lax.rem(c + k, C) for k in range(1, C)]
     z_devices = [{"grp": t} for t in z_peers]
+    x_devices = [{"band": t} for t in x_peers]
     c_devices = [{"half": t} for t in c_peers]
     far_devices = [{"grp": t, "half": u} for t in z_peers for u in c_peers]
-    everyone = z_devices + c_devices + far_devices + [{"band": t} for t in x_peers]
+    everyone = z_devices + c_devices + far_devices + x_devices
     for peer in everyone:
         pl.semaphore_signal(barrier, inc=1, device_id=peer, device_id_type=MESH)
 
-    width = X * S * NB
+    width = slots * BD
     per_tile = 128 // width
     mine_info = z * C + c
     lane = lax.broadcasted_iota(jnp.int32, (8, 128), 1)
     row = lax.broadcasted_iota(jnp.int32, (8, 128), 0)
     first_lane = lax.rem(mine_info, per_tile) * width
-    slot_at = lane // NB - first_lane // NB
+    slot_at = lane // BD - first_lane // BD
     keys = jnp.zeros((8, 128), jnp.int32)
     for xx in range(X):
         for s in range(S):
             group = pair_ref[xx * ppd + s % ppd, s // ppd]
-            keys = jnp.where(slot_at == xx * S + s, group * NB + lane % NB, keys)
+            keys = jnp.where(slot_at == xx * S + s, group * BD + lane % BD, keys)
     columns = jnp.full((8, 128), -1, jnp.int32)
-    band_of = lax.broadcasted_iota(jnp.int32, (S * NB, 128), 0)
-    own_key = jnp.zeros((S * NB, 128), jnp.int32)
+    band_of = lax.broadcasted_iota(jnp.int32, (slots * BD, 128), 0)
+    own_key = jnp.zeros((slots * BD, 128), jnp.int32)
     for s in range(S):
         group = jnp.int32(0)
         for xx in range(X):
-            group = jnp.where(x == xx, pair_ref[xx * ppd + s % ppd, s // ppd], group)
+            here = pair_ref[xx * ppd + s % ppd, s // ppd]
+            group = jnp.where(x == xx, here, group)
+            own_key = jnp.where(band_of // BD == xx * S + s, here * BD + band_of % BD, own_key)
         columns = jnp.where(row == s, group, columns)
-        own_key = jnp.where(band_of // NB == s, group * NB + band_of % NB, own_key)
     info[mine_info] = jnp.where(row == 7, keys, columns)
 
     pl.semaphore_wait(barrier, len(everyone))
@@ -119,48 +123,82 @@
             copy.start()
             row_copies.append(copy)
 
+    def over_band(buffer, send, recv):
+        copies = [
+            pltpu.make_async_remote_copy(
+                src_ref=buffer.at[x],
+                dst_ref=buffer.at[x],
+                send_sem=send.at[n],
+                recv_sem=recv.at[x],
+                device_id=peer,
+                device_id_type=MESH,
+            )
+            for n, peer in enumerate(x_devices)
+        ]
+        for copy in copies:
+            copy.start()
+        return copies
+
+    def from_band(buffer, send, recv):
+        for t in x_peers:
+            pltpu.make_async_remote_copy(
+                src_ref=buffer.at[t],
+                dst_ref=buffer.at[t],
+                send_sem=send.at[0],
+                recv_sem=recv.at[t],
+                device_id=everyone[0],
+                device_id_type=MESH,
+            ).wait_recv()
+
+    band_copies = []
+
     def arrived(half):
         rows = rows_out[half, z]
         for k in range(1, Z):
             row_copies[half * (Z - 1) + k - 1].wait_recv()
             rows = rows + rows_in[half, k - 1]
-        return rows
-
-    band_col = lax.broadcasted_iota(jnp.int32, (NB, 1), 0)
-
-    def table_column(ref, m):
-        column = jnp.zeros((NB, 1), F32)
-        for b in range(NB):
-            column = jnp.where(band_col == b, ref[m, b], column)
+        rows_all[half, x] = rows
+        band_copies.extend(over_band(rows_all.at[half], all_send.at[half], all_recv.at[half]))
+
+    band_col = lax.broadcasted_iota(jnp.int32, (BD, 1), 0)
+
+    def own_column(ref, m):
+        column = jnp.zeros((BD, 1), F32)
+        for b in range(BD):
+            value = ref[m, b]
+            for xx in range(1, X):
+                value = jnp.where(x == xx, ref[m, xx * BD + b], value)
+            column = jnp.where(band_col == b, value, column)
         return column
 
-    share_cols = [table_column(share_ref, m) for m in range(NM)]
-    emis_cols = [table_column(emis_ref, k) for k in range(NCLS)]
-    rows = arrived(0)
-    weights, emis_slots, emit_sums = [], [], []
-    for s in range(S):
-        ids = rows[s : s + 1, :]
-        emis = jnp.broadcast_to(emis_cols[0], (NB, FG))
+    share_cols = [own_column(share_ref, m) for m in range(NM)]
+    emis_cols = [own_column(emis_ref, k) for k in range(NCLS)]
+    arrived(0)
+    from_band(rows_all.at[0], all_send.at[0], all_recv.at[0])
+    weights, emis_slots = [], []
+    for n in range(slots):
+        xx, s = n // S, n % S
+        ids = rows_all[0, xx, s : s + 1, :]
+        emis = jnp.broadcast_to(emis_cols[0], (BD, FG))
         material = ids
         for k in range(1, NCLS):
             emis = jnp.where(ids > k * NM - 0.5, emis_cols[k], emis)
             material = jnp.where(ids > k * NM - 0.5, ids - k * NM, material)
-        share = jnp.broadcast_to(share_cols[0], (NB, FG))
+        share = jnp.broadcast_to(share_cols[0], (BD, FG))
         for m in range(1, NM):
             share = jnp.where(material > m - 0.5, share_cols[m], share)
         weight = emis * share
         weights.append(weight)
         emis_slots.append(emis)
-        emit_sums.append(jnp.sum(weight, axis=0, keepdims=True))
-        rad[s] = (weight * rows[S + s : S + s + 1, :]).astype(BF16)
+        rad[n] = weight * rows_all[0, xx, S + s : S + s + 1, :]
     load_kern.wait()
 
-    def block_of(zz, xx, cc):
-        return (zz * C + cc) * X + xx
-
-    rows_block = S * NB
+    def block_of(zz, cc):
+        return zz * C + cc
+
+    rows_block = slots * BD
     for sweep in range(SWEEPS):
-        mine = block_of(z, x, c)
+        mine = block_of(z, c)
         started = []
         final = sweep == SWEEPS - 1
         buffer = last if final else gath.at[sweep]
@@ -187,44 +225,41 @@
                 device_id_type=pl.DeviceIdType.MESH,
             ).wait_recv()
 
-        to_first, to_second = [], []
-        for q in range(ppd):
-            to_first.append(
-                lax.dot_general(
-                    rad[ppd + q], kern[q], (((1,), (1,)), ((), ())), preferred_element_type=F32
+        for n in range(slots):
+            xx, end, q = n // S, n % S // ppd, n % ppd
+            pair = kern[xx * ppd + q]
+            if end == 0:
+                term = lax.dot_general(
+                    rad[n + ppd].astype(BF16), pair, (((1,), (1,)), ((), ())), preferred_element_type=F32
                 )
-            )
-            to_second.append(jnp.dot(rad[q], kern[q], preferred_element_type=F32))
-        buffer[mine] = jnp.concatenate(to_first + to_second, axis=0).astype(buffer.dtype)
-
-        for t in z_peers:
-            send(mine, {"grp": t})
-        for t in x_peers:
-            send(mine, {"band": t})
-        for t in c_peers:
-            send(mine, {"half": t})
-        for xt in x_peers:
-            block = block_of(z, xt, c)
-            receive(block)
-            for t in c_peers:
-                send(block, {"half": t})
+            else:
+                term = jnp.dot(rad[n - ppd].astype(BF16), pair, preferred_element_type=F32)
+            stage[n * BD : (n + 1) * BD, :] = term
+        buffer[mine] = stage[...].astype(buffer.dtype)
+
+        for peer in z_devices + c_devices:
+            send(mine, peer)
+        if not final:
+            arrived(1)
+            emit_sums = []
+            for n in range(slots):
+                ids = rows_all[0, n // S, n % S : n % S + 1, :]
+                emit_sum = jnp.zeros((1, FG), F32)
+                for k in range(NCLS):
+                    for m in range(NM):
+                        total = emis_ref[k, 0] * share_ref[m, 0]
+                        for b in range(1, NB):
+                            total = total + emis_ref[k, b] * share_ref[m, b]
+                        emit_sum = jnp.where(ids > k * NM + m - 0.5, total, emit_sum)
+                emit_sums.append(emit_sum)
+            from_band(rows_all.at[1], all_send.at[1], all_recv.at[1])
         for zt in z_peers:
-            block = block_of(zt, x, c)
-            receive(block)
-            for t in x_peers:
-                send(block, {"band": t})
-            for t in c_peers:
-                send(block, {"half": t})
-        for zt in z_peers:
-            for xt in x_peers:
-                block = block_of(zt, xt, c)
-                receive(block)
-                for t in c_peers:
-                    send(block, {"half": t})
+            receive(block_of(zt, c))
+            for peer in c_devices:
+                send(block_of(zt, c), peer)
         for ct in c_peers:
             for zt in [z] + z_peers:
-                for xt in [x] + x_peers:
-                    receive(block_of(zt, xt, ct))
+                receive(block_of(zt, ct))
 
         if sweep == 0:
             for t in z_peers + [z]:
@@ -237,30 +272,51 @@
                     tile = tile + info[t * per_tile + n]
                 tiles.append(tile[7:8, :])
             key_row = jnp.concatenate(tiles, axis=1)
-            area_rows = arrived(1)
 
         terms = buffer[...].reshape(-1, FG)
         count = terms.shape[0]
         if not final:
             select = jnp.where(own_key[:, :1] == key_row, jnp.ones((rows_block, count), F32), 0.0)
             incoming = jnp.dot(select.astype(BF16), terms, preferred_element_type=F32)
-            for s in range(S):
-                emis = emis_slots[s]
-                irradiance = incoming[s * NB : (s + 1) * NB, :] / area_rows[s : s + 1, :]
-                absorbed = jnp.sum(emis * irradiance, axis=0, keepdims=True)
-                fourth = (absorbed + area_rows[S + s : S + s + 1, :]) / emit_sums[s]
-                rad[s] = (weights[s] * fourth + (1.0 - emis) * irradiance).astype(BF16)
+            stage[...] = incoming
+            for n in range(slots):
+                xx, s = n // S, n % S
+                irradiance = stage[n * BD : (n + 1) * BD, :] / rows_all[1, xx, s : s + 1, :]
+                stage[n * BD : (n + 1) * BD, :] = irradiance
+                sum_first[x, n : n + 1, :] = jnp.sum(emis_slots[n] * irradiance, axis=0, keepdims=True)
+            band_copies.extend(over_band(sum_first, sum_send.at[0], sum_recv.at[0]))
+            from_band(sum_first, sum_send.at[0], sum_recv.at[0])
+            absorbed = sum_first[0]
+            for xx in range(1, X):
+                absorbed = absorbed + sum_first[xx]
+            for n in range(slots):
+                xx, s = n // S, n % S
+                fourth = (absorbed[n : n + 1, :] + rows_all[1, xx, S + s : S + s + 1, :]) / emit_sums[n]
+                irradiance = stage[n * BD : (n + 1) * BD, :]
+                rad[n] = weights[n] * fourth + (1.0 - emis_slots[n]) * irradiance
         else:
-            row_key = lax.broadcasted_iota(jnp.int32, (groups_dev * NB, count), 0) + z * (groups_dev * NB)
+            row_key = lax.broadcasted_iota(jnp.int32, (groups_dev * BD, count), 0) + z * (groups_dev * BD)
             select = jnp.where(row_key == key_row, jnp.ones(row_key.shape, F32), 0.0).astype(BF16)
             high = terms.astype(BF16)
             low = (terms - high.astype(F32)).astype(BF16)
             inc_ref[...] = jnp.dot(select, high, preferred_element_type=F32) + jnp.dot(
                 select, low, preferred_element_type=F32
             )
+            for g in range(groups_dev):
+                emis = emis_cols[0]
+                for k in range(1, NCLS):
+                    emis = jnp.where(coat_ref[g] == k, emis_cols[k], emis)
+                received = emis * inc_ref[g * BD : (g + 1) * BD, :]
+                sum_last[x, g : g + 1, :] = jnp.sum(received, axis=0, keepdims=True) / held[1, g : g + 1, :]
+            band_copies.extend(over_band(sum_last, sum_send.at[1], sum_recv.at[1]))
+            from_band(sum_last, sum_send.at[1], sum_recv.at[1])
+            absorbed = sum_last[0]
+            for xx in range(1, X):
+                absorbed = absorbed + sum_last[xx]
+            absorbed_ref[...] = absorbed
         for copy in started:
             copy.wait_send()
-    for copy in info_copies + row_copies:
+    for copy in info_copies + row_copies + band_copies:
         copy.wait_send()
 
 
@@ -275,7 +331,7 @@
     pairs_dev = pair_list.shape[0]
     ppd = pairs_dev // X
     S = 2 * ppd
-    D = Z * X * C
+    D = Z * C
     bands_dev = NB // X
 
     def emis_of(classes):
@@ -286,21 +342,28 @@
 
     smem = pl.BlockSpec(memory_space=pltpu.SMEM)
     dma = pltpu.SemaphoreType.DMA
-    incoming = pl.pallas_call(
+    incoming, absorbed = pl.pallas_call(
         functools.partial(exchange, (Z, X, C, S, ppd, NB, NM, NCLS)),
-        out_shape=jax.ShapeDtypeStruct((groups_dev * NB, FG), F32),
+        out_shape=(
+            jax.ShapeDtypeStruct((groups_dev * bands_dev, FG), F32),
+            jax.ShapeDtypeStruct((groups_dev, FG), F32),
+        ),
         in_specs=[smem] * 4 + [pl.BlockSpec(memory_space=pl.ANY)] * 5,
-        out_specs=pl.BlockSpec(memory_space=pltpu.VMEM),
+        out_specs=(pl.BlockSpec(memory_space=pltpu.VMEM),) * 2,
         scratch_shapes=[
             pltpu.VMEM((3, groups_dev, FG), F32),
             pltpu.VMEM((groups_dev, FG), jnp.int32),
-            pltpu.VMEM((ppd, FG, FG), BF16),
+            pltpu.VMEM((pairs_dev, FG, FG), BF16),
             pltpu.VMEM((Z * C, 8, 128), jnp.int32),
             pltpu.VMEM((2, Z, 2 * S, FG), F32),
             pltpu.VMEM((2, Z - 1, 2 * S, FG), F32),
-            pltpu.VMEM((S, NB, FG), BF16),
-            pltpu.VMEM((SWEEPS - 1, D, S * NB, FG), BF16),
-            pltpu.VMEM((D, S * NB, FG), F32),
+            pltpu.VMEM((2, X, 2 * S, FG), F32),
+            pltpu.VMEM((2 * pairs_dev, bands_dev, FG), F32),
+            pltpu.VMEM((2 * pairs_dev * bands_dev, FG), F32),
+            pltpu.VMEM((SWEEPS - 1, D, 2 * pairs_dev * bands_dev, FG), BF16),
+            pltpu.VMEM((D, 2 * pairs_dev * bands_dev, FG), F32),
+            pltpu.VMEM((X, 2 * pairs_dev, FG), F32),
+            pltpu.VMEM((X, groups_dev, FG), F32),
             dma((3,)),
             dma(()),
             dma(()),
@@ -308,11 +371,15 @@
             dma((Z * C,)),
             dma((2, Z - 1)),
             dma((2, Z - 1)),
-            dma((SWEEPS, D)),
+            dma((2, X - 1)),
+            dma((2, X)),
+            dma((2, X - 1)),
+            dma((2, X)),
+            dma((SWEEPS, 2 * D)),
             dma((SWEEPS, D)),
         ],
         compiler_params=pltpu.CompilerParams(
-            collective_id=0, has_side_effects=True, vmem_limit_bytes=48 * 1024 * 1024
+            collective_id=0, has_side_effects=True, vmem_limit_bytes=60 * 1024 * 1024
         ),
         cost_estimate=pl.CostEstimate(flops=200_000_000, bytes_accessed=8_000_000, transcendentals=0),
     )(
@@ -326,8 +393,6 @@
         share = jnp.where((material == m)[:, None, :], share_table[m][None, :, None], share)
     weight = emis * share
     emit_sum = jnp.sum(weight, axis=1)
-    irradiance = incoming.reshape(groups_dev, NB, FG) / facet_areas[:, None, :]
-    absorbed = jnp.sum(emis * irradiance, axis=1)
     fourth = (absorbed + heat_load) / emit_sum
 
     def mine(rows):
@@ -338,7 +403,7 @@
     for m in range(NM):
         share_mine = jnp.where((material == m)[:, None, :], table[m][None, :, None], share_mine)
     emis_mine = mine(emis)
-    incoming_mine = mine(incoming.reshape(groups_dev, NB, FG))
+    incoming_mine = incoming.reshape(groups_dev, bands_dev, FG)
     radiosity = emis_mine * share_mine * fourth[:, None, :] + (1.0 - emis_mine) * (
         incoming_mine / facet_areas[:, None, :]
     )

time: 71.6 us -> 63.5 us (0.89)
  local copies, waits for them, and re-layouts: 8.98 us -> 2.72 us
  other arithmetic: 6.22 us -> 5.22 us
    unnamed x15 -> x13, local copies, waits for them, and re-layouts: 6.4 us -> 1.44 us
    reshape x0 -> x1, local copies, waits for them, and re-layouts: none -> 1.19 us  [on_device(): incoming_mine = incoming.reshape(groups_dev, bands_dev, FG)]
    broadcast_in_dim x1, local copies, waits for them, and re-layouts: 0.98 us -> 0.01 us  [on_device(): jnp.where((material == m)[:, None, :], share_table[m][None, :, None], share)]
    pow x1, other arithmetic: 0.73 us -> 1.63 us  [on_device(): return (radiosity.astype(BF16), fourth ** 0.25)]
    eq x1, other arithmetic: 1.06 us -> 0.16 us  [on_device(): material == m]
    broadcast_in_dim x1, local copies, waits for them, and re-layouts: 0.83 us -> 0.01 us  [emis_of(): result = jnp.where((classes == k)[:, None], emis_table[k][None, :], result)]
where the time goes in v1:
time: 63.5 us; the launch traced here: 63.3 us
  Pallas kernels  54.6 us (86%)
  other arithmetic  5.22 us (8%)
  local copies, waits for them, and re-layouts  2.72 us (4%)
  between operations  0.77 us (1%)
    pallas_call x1, Pallas kernels, on_device(): pl.pallas_call(functools.partial(exchange, (Z, X, C, S, ppd, NB, NM, NCLS...  54.6 us
    convert_element_type x1, other arithmetic, on_device(): return (radiosity.astype(BF16), fourth ** 0.25)  1.97 us
    pow x1, other arithmetic, on_device(): return (radiosity.astype(BF16), fourth ** 0.25)  1.63 us
    unnamed x13, local copies, waits for them, and re-layouts  1.44 us
    reduce_sum x1, other arithmetic, on_device(): emit_sum = jnp.sum(weight, axis=1)  1.3 us

profile of v1, /device:TPU:9, one launch (start us, length us, event | category | flops | bytes accessed | tf_op | source)
XLA Modules:
  0.0 63.3 jit_solution(7639210217551912360)
XLA Ops:
  0.6 0.0 copy-start.5
  0.6 0.0 copy-start.4
  0.7 0.0 copy-start.3
  0.7 0.0 copy-start
  0.7 0.0 copy-start.2
  0.7 0.0 copy-start.1
  0.7 1.4 %copy.12.refs_0_ = s32[4,2]{1,0:T(4,128)} copy(s32[4,2]{0,1:T(2,128)} %param.9) | data formatting | bytes 64 | tf_op args[0]
  2.1 54.6 %shard_map.104 = (f32[128,1024]{1,0:T(8,128)}, f32[32,1024]{1,0:T(8,128)}) custom-call(s32[4,2]{1,0:T(4,128)} %copy.12.refs_0_, s32[32]{0:T(128)} %refs_1_.1, f32[4,8]{1,0:T(4,128)} %refs_2_.1, f32[8,8]{1,0:T(8,128)} %refs_3_.1, s32[32,1024]{1,0:T(8,128)} %refs_4_.1, f32[32,1024]{1,0:T(8,128)} %refs_5_.1, f32[32,1024]{1,0:T(8,128)} %refs_6_.1, ...), custom_call_target="tpu_custom_call" | custom-call | flops 200000000 | bytes 8000000 | tf_op jit(solution)/shard_map/pallas_call | solution.py:345
  56.7 1.2 %reshape.149 = f32[32,4,1024]{2,1,0:T(4,128)S(1)} reshape(f32[128,1024]{1,0:T(8,128)} %get-tuple-element.5) | data formatting | bytes 1048576 | tf_op jit(solution)/shard_map/reshape | solution.py:406
  57.9 0.0 copy-done.4
  57.9 0.0 copy-done.5
  57.9 0.1 select_select_fusion
  58.0 0.1 broadcast_subtract_fusion
  58.1 0.0 copy-done.3
  58.1 0.0 copy-done
  58.1 0.2 broadcast_compare_fusion.7
  58.3 1.3 %multiply_reduce_fusion = f32[32,1024]{1,0:T(8,128)S(1)} fusion(f32[8]{0:T(128)S(1)} %get-tuple-element.32, f32[8]{0:T(128)S(1)} %get-tuple-element.33, f32[8]{0:T(128)S(1)} %get-tuple-element.27, f32[8]{0:T(128)S(1)} %get-tuple-element.28, f32[8]{0:T(128)S(1)} %get-tuple-element.29, f32[8]{0:T(128)S(1)} %get-tuple-element.30, f32[8]{0:T(128)S(1)} %get-tuple-element.31, ...), kind=kLoop, calls=%fused_computation | loop fusion | flops 2588672 | bytes 394496 | tf_op jit(solution)/shard_map/reduce_sum | solution.py:395
  59.6 0.0 copy-done.1
  59.6 1.6 %broadcast_power_fusion = (f32[32,1024]{1,0:T(8,128)}, f32[32,1024]{1,0:T(8,128)S(1)}) fusion(f32[32,1024]{1,0:T(8,128)S(1)} %multiply_reduce_fusion, f32[32,1024]{1,0:T(8,128)} %get-tuple-element.4, f32[32,1024]{1,0:T(8,128)S(1)} %copy-done.1), kind=kLoop, calls=%fused_computation.3 | loop fusion | flops 65536 | bytes 655360 | tf_op jit(solution)/shard_map/pow | solution.py:410
  61.2 0.1 constant_dynamic-slice_fusion
  61.3 0.0 copy-done.2
  61.3 2.0 %add_convert_fusion = bf16[32,4,1024]{2,1,0:T(4,128)(2,1)} fusion(f32[32,4,1024]{2,1,0:T(4,128)S(1)} %reshape.149, f32[32,1024]{1,0:T(8,128)S(1)} %copy-done.2, f32[32,4]{1,0:T(8,128)S(1)} %get-tuple-element.8, f32[32,1024]{1,0:T(8,128)S(1)} %get-tuple-element.7, f32[4]{0:T(128)S(1)} %get-tuple-element.19, f32[4]{0:T(128)S(1)} %get-tuple-element.20, ...), kind=kLoop, calls=%fused_computation.1 | loop fusion | flops 1835008 | bytes 1311872 | tf_op jit(solution)/shard_map/convert_element_type | solution.py:410
  (4 shorter events, 0.0 us)
Async XLA Ops:
  0.6 57.3 %copy-start.5 = (s32[32]{0:T(128)S(1)}, s32[32]{0:T(128)}, u32[]{:S(2)}) copy-start(s32[32]{0:T(128)} %refs_1_.1) | copy-start | bytes 388
  0.6 57.2 %copy-start.4 = (f32[4,8]{1,0:T(4,128)S(1)}, f32[4,8]{1,0:T(4,128)}, u32[]{:S(2)}) copy-start(f32[4,8]{1,0:T(4,128)} %refs_2_.1) | copy-start | bytes 388
  0.7 57.4 %copy-start.3 = (f32[8,8]{1,0:T(8,128)S(1)}, f32[8,8]{1,0:T(8,128)}, u32[]{:S(2)}) copy-start(f32[8,8]{1,0:T(8,128)} %refs_3_.1) | copy-start | bytes 772
  0.7 57.4 %copy-start = (s32[32,1024]{1,0:T(8,128)S(1)}, s32[32,1024]{1,0:T(8,128)}, u32[]{:S(2)}) copy-start(s32[32,1024]{1,0:T(8,128)} %refs_4_.1) | copy-start | bytes 393220
  0.7 60.6 %copy-start.2 = (f32[32,1024]{1,0:T(8,128)S(1)}, f32[32,1024]{1,0:T(8,128)}, u32[]{:S(2)}) copy-start(f32[32,1024]{1,0:T(8,128)} %refs_6_.1) | copy-start | bytes 393220
  0.7 58.9 %copy-start.1 = (f32[32,1024]{1,0:T(8,128)S(1)}, f32[32,1024]{1,0:T(8,128)}, u32[]{:S(2)}) copy-start(f32[32,1024]{1,0:T(8,128)} %refs_7_.1) | copy-start | bytes 393220

commit v2 on v1

--- a/solution.py
+++ b/solution.py
@@ -17,8 +17,8 @@
     slots, BD = X * S, NB // X
     (
         pair_ref, coat_ref, emis_ref, share_ref,
-        mat_hbm, start_hbm, areas_hbm, heat_hbm, kern_hbm, inc_ref, absorbed_ref,
-        held, mats, kern, info, rows_out, rows_in, rows_all, rad, stage, gath, last, sum_first, sum_last,
+        mat_hbm, start_hbm, areas_hbm, heat_hbm, kern_hbm, inc_ref, fourth_ref,
+        held, mats, ident, kern, info, rows_out, rows_in, rows_all, rad, stage, gath, last, sum_first, sum_last, emit_held, inc_all,
         held_sem, mat_sem, kern_sem, info_send, info_recv, row_send, row_recv,
         all_send, all_recv, sum_send, sum_recv, send_sem, recv_sem,
     ) = refs
@@ -95,20 +95,28 @@
         coat = jnp.where(group_row == g, coat_ref[g], coat)
     for load in loads:
         load.wait()
-    combined = (coat * NM + mats[...]).astype(F32)
+    ident[...] = (coat * NM + mats[...]).astype(F32)
     for t in z_peers:
         info_copy(0, t * C + c, everyone[0]).wait_recv()
 
     want = jnp.concatenate([info[t * C + c] for t in range(Z)], axis=0)[:, :groups_dev]
     local = lax.broadcasted_iota(jnp.int32, (Z * 8, groups_dev), 1) + z * groups_dev
     pick = jnp.where(want == local, jnp.ones(want.shape, F32), 0.0)
+    pick3 = jnp.concatenate([pick] * 3, axis=1).astype(BF16)
+    pick = pick.astype(BF16)
     row_copies = []
     for half in range(2):
         for a in range(2):
-            source = combined if half + a == 0 else held[half * 2 + a - 1]
-            found = jnp.dot(
-                pick, source, precision=lax.Precision.HIGHEST, preferred_element_type=F32
-            )
+            if half + a == 0:
+                found = jnp.dot(pick, ident[...].astype(BF16), preferred_element_type=F32)
+            else:
+                source = held[half * 2 + a - 1]
+                high = source.astype(BF16)
+                rest = source - high.astype(F32)
+                middle = rest.astype(BF16)
+                low = (rest - middle.astype(F32)).astype(BF16)
+                parts = jnp.concatenate([high, middle, low], axis=0)
+                found = jnp.dot(pick3, parts, preferred_element_type=F32)
             for t in range(Z):
                 rows_out[half, t, a * S : (a + 1) * S, :] = found[t * 8 : t * 8 + S, :]
         for k in range(1, Z):
@@ -196,6 +204,20 @@
     def block_of(zz, cc):
         return zz * C + cc
 
+    totals = []
+    for k in range(NCLS):
+        for m in range(NM):
+            total = emis_ref[k, 0] * share_ref[m, 0]
+            for b in range(1, NB):
+                total = total + emis_ref[k, b] * share_ref[m, b]
+            totals.append(total)
+
+    def emit_of(ids):
+        emit_sum = jnp.full(ids.shape, totals[0], F32)
+        for n in range(1, len(totals)):
+            emit_sum = jnp.where(ids > n - 0.5, totals[n], emit_sum)
+        return emit_sum
+
     rows_block = slots * BD
     for sweep in range(SWEEPS):
         mine = block_of(z, c)
@@ -241,18 +263,11 @@
             send(mine, peer)
         if not final:
             arrived(1)
-            emit_sums = []
-            for n in range(slots):
-                ids = rows_all[0, n // S, n % S : n % S + 1, :]
-                emit_sum = jnp.zeros((1, FG), F32)
-                for k in range(NCLS):
-                    for m in range(NM):
-                        total = emis_ref[k, 0] * share_ref[m, 0]
-                        for b in range(1, NB):
-                            total = total + emis_ref[k, b] * share_ref[m, b]
-                        emit_sum = jnp.where(ids > k * NM + m - 0.5, total, emit_sum)
-                emit_sums.append(emit_sum)
+            emit_rows = [emit_of(rows_all[0, xx, :S, :]) for xx in range(X)]
+            emit_sums = [emit_rows[n // S][n % S : n % S + 1, :] for n in range(slots)]
             from_band(rows_all.at[1], all_send.at[1], all_recv.at[1])
+        else:
+            emit_held[...] = emit_of(ident[...])
         for zt in z_peers:
             receive(block_of(zt, c))
             for peer in c_devices:
@@ -299,21 +314,23 @@
             select = jnp.where(row_key == key_row, jnp.ones(row_key.shape, F32), 0.0).astype(BF16)
             high = terms.astype(BF16)
             low = (terms - high.astype(F32)).astype(BF16)
-            inc_ref[...] = jnp.dot(select, high, preferred_element_type=F32) + jnp.dot(
+            inc_all[...] = jnp.dot(select, high, preferred_element_type=F32) + jnp.dot(
                 select, low, preferred_element_type=F32
             )
             for g in range(groups_dev):
                 emis = emis_cols[0]
                 for k in range(1, NCLS):
                     emis = jnp.where(coat_ref[g] == k, emis_cols[k], emis)
-                received = emis * inc_ref[g * BD : (g + 1) * BD, :]
+                piece = inc_all[g * BD : (g + 1) * BD, :]
+                received = emis * piece
+                inc_ref[g] = piece
                 sum_last[x, g : g + 1, :] = jnp.sum(received, axis=0, keepdims=True) / held[1, g : g + 1, :]
             band_copies.extend(over_band(sum_last, sum_send.at[1], sum_recv.at[1]))
             from_band(sum_last, sum_send.at[1], sum_recv.at[1])
             absorbed = sum_last[0]
             for xx in range(1, X):
                 absorbed = absorbed + sum_last[xx]
-            absorbed_ref[...] = absorbed
+            fourth_ref[...] = (absorbed + held[2]) / emit_held[...]
         for copy in started:
             copy.wait_send()
     for copy in info_copies + row_copies + band_copies:
@@ -342,10 +359,10 @@
 
     smem = pl.BlockSpec(memory_space=pltpu.SMEM)
     dma = pltpu.SemaphoreType.DMA
-    incoming, absorbed = pl.pallas_call(
+    incoming, fourth = pl.pallas_call(
         functools.partial(exchange, (Z, X, C, S, ppd, NB, NM, NCLS)),
         out_shape=(
-            jax.ShapeDtypeStruct((groups_dev * bands_dev, FG), F32),
+            jax.ShapeDtypeStruct((groups_dev, bands_dev, FG), F32),
             jax.ShapeDtypeStruct((groups_dev, FG), F32),
         ),
         in_specs=[smem] * 4 + [pl.BlockSpec(memory_space=pl.ANY)] * 5,
@@ -353,6 +370,7 @@
         scratch_shapes=[
             pltpu.VMEM((3, groups_dev, FG), F32),
             pltpu.VMEM((groups_dev, FG), jnp.int32),
+            pltpu.VMEM((groups_dev, FG), F32),
             pltpu.VMEM((pairs_dev, FG, FG), BF16),
             pltpu.VMEM((Z * C, 8, 128), jnp.int32),
             pltpu.VMEM((2, Z, 2 * S, FG), F32),
@@ -364,6 +382,8 @@
             pltpu.VMEM((D, 2 * pairs_dev * bands_dev, FG), F32),
             pltpu.VMEM((X, 2 * pairs_dev, FG), F32),
             pltpu.VMEM((X, groups_dev, FG), F32),
+            pltpu.VMEM((groups_dev, FG), F32),
+            pltpu.VMEM((groups_dev * bands_dev, FG), F32),
             dma((3,)),
             dma(()),
             dma(()),
@@ -388,12 +408,6 @@
     )
 
     emis = emis_of(coating)[:, :, None]
-    share = jnp.zeros((groups_dev, NB, FG), F32)
-    for m in range(NM):
-        share = jnp.where((material == m)[:, None, :], share_table[m][None, :, None], share)
-    weight = emis * share
-    emit_sum = jnp.sum(weight, axis=1)
-    fourth = (absorbed + heat_load) / emit_sum
 
     def mine(rows):
         return lax.dynamic_slice_in_dim(rows, x * bands_dev, bands_dev, 1)
@@ -403,9 +417,8 @@
     for m in range(NM):
         share_mine = jnp.where((material == m)[:, None, :], table[m][None, :, None], share_mine)
     emis_mine = mine(emis)
-    incoming_mine = incoming.reshape(groups_dev, bands_dev, FG)
     radiosity = emis_mine * share_mine * fourth[:, None, :] + (1.0 - emis_mine) * (
-        incoming_mine / facet_areas[:, None, :]
+        incoming / facet_areas[:, None, :]
     )
     return (radiosity.astype(BF16), fourth**0.25)
 

time: 63.5 us -> 65.2 us (1.027)
  local copies, waits for them, and re-layouts: 2.72 us -> 4.88 us
    pow x1 -> x0, other arithmetic: 1.63 us -> none  [on_device(): return (radiosity.astype(BF16), fourth ** 0.25)]
    pow x0 -> x1, local copies, waits for them, and re-layouts: none -> 1.61 us  [on_device(): return (radiosity.astype(BF16), fourth ** 0.25)]
    reduce_sum x1 -> x0, other arithmetic: 1.3 us -> none  [on_device(): emit_sum = jnp.sum(weight, axis=1)]
    reshape x1 -> x0, local copies, waits for them, and re-layouts: 1.19 us -> none  [on_device(): incoming_mine = incoming.reshape(groups_dev, bands_dev, FG)]
    convert_element_type x1, other arithmetic: 1.97 us -> 3.02 us  [on_device(): return (radiosity.astype(BF16), fourth ** 0.25)]
    eq x1, other arithmetic: 0.16 us -> 1.06 us  [on_device(): material == m]
    broadcast_in_dim x1, local copies, waits for them, and re-layouts: 0.01 us -> 0.83 us  [emis_of(): result = jnp.where((classes == k)[:, None], emis_table[k][None, :], result)]
    dynamic_slice x1, local copies, waits for them, and re-layouts: 0.07 us -> 0.76 us  [mine(): return lax.dynamic_slice_in_dim(rows, x * bands_dev, bands_dev, 1)]
where the time goes in v2:
time: 65.2 us; the launch traced here: 64.9 us
  Pallas kernels  54.5 us (84%)
  local copies, waits for them, and re-layouts  4.88 us (7%)
  other arithmetic  4.82 us (7%)
  between operations  0.67 us (1%)
    pallas_call x1, Pallas kernels, on_device(): pl.pallas_call(functools.partial(exchange, (Z, X, C, S, ppd, NB, NM, NCLS...  54.5 us
    convert_element_type x1, other arithmetic, on_device(): return (radiosity.astype(BF16), fourth ** 0.25)  3.02 us
    pow x1, local copies, waits for them, and re-layouts, on_device(): return (radiosity.astype(BF16), fourth ** 0.25)  1.61 us
    unnamed x3, local copies, waits for them, and re-layouts  1.38 us

profile of v2, /device:TPU:9, one launch (start us, length us, event | category | flops | bytes accessed | tf_op | source)
XLA Modules:
  0.0 64.9 jit_solution(5918080856626779707)
XLA Ops:
  0.6 0.0 copy-start
  0.6 1.4 %copy.11.refs_0_ = s32[4,2]{1,0:T(4,128)} copy(s32[4,2]{0,1:T(2,128)} %param.9) | data formatting | bytes 64 | tf_op args[0]
  2.0 0.7 %broadcast_compare_fusion.11 = (pred[32]{0:T(512)(128)(4,1)S(1)}, pred[32]{0:T(512)(128)(4,1)S(1)}, pred[32]{0:T(512)(128)(4,1)S(1)}, pred[32]{0:T(512)(128)(4,1)S(1)}) fusion(s32[32]{0:T(128)} %refs_1_.1), kind=kLoop, calls=%fused_computation.28 | loop fusion | flops 128 | bytes 256 | tf_op jit(solution)/shard_map/eq | solution.py:357
  2.7 0.8 %slice_bitcast_fusion.11 = (f32[8]{0:T(128)S(1)}, f32[8]{0:T(128)S(1)}, f32[8]{0:T(128)S(1)}, f32[8]{0:T(128)S(1)}) fusion(f32[4,8]{1,0:T(4,128)} %refs_2_.1), kind=kLoop, calls=%fused_computation.23 | loop fusion | bytes 256 | tf_op jit(solution)/shard_map/jit(_where)/broadcast_in_dim | solution.py:357
  3.5 0.1 dynamic-slice.7
  3.6 0.1 dynamic-slice.5
  3.7 0.1 dynamic-slice.6
  3.7 0.1 dynamic-slice.4
  3.8 0.8 %constant_dynamic-slice_fusion = f32[8,4]{1,0:T(8,128)S(1)} fusion(f32[8,8]{1,0:T(8,128)} %refs_3_.1, s32[]{:T(128)S(6)} %select_n.46), kind=kLoop, calls=%fused_computation.25 | loop fusion | bytes 260 | tf_op jit(solution)/shard_map/dynamic_slice | solution.py:413
  4.6 0.1 select_select_fusion
  4.7 1.1 %broadcast_compare_fusion.7 = (pred[32,1024]{1,0:T(8,128)(4,1)S(1)}, pred[32,1024]{1,0:T(8,128)(4,1)S(1)}, pred[32,1024]{1,0:T(8,128)(4,1)S(1)}, pred[32,1024]{1...) fusion(s32[32,1024]{1,0:T(8,128)} %refs_4_.1), kind=kLoop, calls=%fused_computation.9 | loop fusion | flops 262144 | bytes 393216 | tf_op jit(solution)/shard_map/eq | solution.py:418
  5.7 54.5 %shard_map.104 = (f32[32,4,1024]{2,1,0:T(4,128)}, f32[32,1024]{1,0:T(8,128)}) custom-call(s32[4,2]{1,0:T(4,128)} %copy.11.refs_0_, s32[32]{0:T(128)} %refs_1_.1, f32[4,8]{1,0:T(4,128)} %refs_2_.1, f32[8,8]{1,0:T(8,128)} %refs_3_.1, s32[32,1024]{1,0:T(8,128)} %refs_4_.1, f32[32,1024]{1,0:T(8,128)} %refs_5_.1, f32[32,1024]{1,0:T(8,128)} %refs_6_.1, ...), custom_call_target="tpu_custom_call" | custom-call | flops 200000000 | bytes 8000000 | tf_op jit(solution)/shard_map/pallas_call | solution.py:362
  60.2 0.0 copy-done
  60.2 3.0 %add_convert_fusion = bf16[32,4,1024]{2,1,0:T(4,128)(2,1)} fusion(f32[32,4,1024]{2,1,0:T(4,128)} %get-tuple-element.5, f32[32,1024]{1,0:T(8,128)S(1)} %copy-done, f32[32,4]{1,0:T(8,128)S(1)} %get-tuple-element.15, f32[32,1024]{1,0:T(8,128)} %get-tuple-element.4, f32[4]{0:T(128)S(1)} %get-tuple-element.17, f32[4]{0:T(128)S(1)} %get-tuple-element.18, ...), kind=kLoop, calls=%fused_computation | loop fusion | flops 1835008 | bytes 1311872 | tf_op jit(solution)/shard_map/convert_element_type | solution.py:423
  63.3 1.6 %broadcast_power_fusion = f32[32,1024]{1,0:T(8,128)} fusion(f32[32,1024]{1,0:T(8,128)} %get-tuple-element.4), kind=kLoop, calls=%fused_computation.1 | loop fusion | bytes 262144 | tf_op jit(solution)/shard_map/pow | solution.py:423
  (1 shorter events, 0.0 us)
Async XLA Ops:
  0.6 59.6 %copy-start = (f32[32,1024]{1,0:T(8,128)S(1)}, f32[32,1024]{1,0:T(8,128)}, u32[]{:S(2)}) copy-start(f32[32,1024]{1,0:T(8,128)} %refs_6_.1) | copy-start | bytes 393220

commit v3 on v2

--- a/solution.py
+++ b/solution.py
@@ -17,8 +17,8 @@
     slots, BD = X * S, NB // X
     (
         pair_ref, coat_ref, emis_ref, share_ref,
-        mat_hbm, start_hbm, areas_hbm, heat_hbm, kern_hbm, inc_ref, fourth_ref,
-        held, mats, ident, kern, info, rows_out, rows_in, rows_all, rad, stage, gath, last, sum_first, sum_last, emit_held, inc_all,
+        mat_hbm, start_hbm, areas_hbm, heat_hbm, kern_hbm, out_ref, fourth_ref,
+        held, mats, ident, kern, info, rows_out, rows_in, rows_all, rad, stage, gath, last, sum_first, sum_last, emit_held, inc_all, weight_held,
         held_sem, mat_sem, kern_sem, info_send, info_recv, row_send, row_recv,
         all_send, all_recv, sum_send, sum_recv, send_sem, recv_sem,
     ) = refs
@@ -170,13 +170,16 @@
 
     band_col = lax.broadcasted_iota(jnp.int32, (BD, 1), 0)
 
+    def own_value(ref, m, b):
+        value = ref[m, b]
+        for xx in range(1, X):
+            value = jnp.where(x == xx, ref[m, xx * BD + b], value)
+        return value
+
     def own_column(ref, m):
         column = jnp.zeros((BD, 1), F32)
         for b in range(BD):
-            value = ref[m, b]
-            for xx in range(1, X):
-                value = jnp.where(x == xx, ref[m, xx * BD + b], value)
-            column = jnp.where(band_col == b, value, column)
+            column = jnp.where(band_col == b, own_value(ref, m, b), column)
         return column
 
     share_cols = [own_column(share_ref, m) for m in range(NM)]
@@ -268,6 +271,16 @@
             from_band(rows_all.at[1], all_send.at[1], all_recv.at[1])
         else:
             emit_held[...] = emit_of(ident[...])
+            emis_held = []
+            for b in range(BD):
+                emis = jnp.full(coat.shape, own_value(emis_ref, 0, b), F32)
+                for k in range(1, NCLS):
+                    emis = jnp.where(coat == k, own_value(emis_ref, k, b), emis)
+                emis_held.append(emis)
+                share = jnp.full(mats.shape, own_value(share_ref, 0, b), F32)
+                for m in range(1, NM):
+                    share = jnp.where(mats[...] == m, own_value(share_ref, m, b), share)
+                weight_held[b] = emis * share
         for zt in z_peers:
             receive(block_of(zt, c))
             for peer in c_devices:
@@ -310,27 +323,31 @@
                 irradiance = stage[n * BD : (n + 1) * BD, :]
                 rad[n] = weights[n] * fourth + (1.0 - emis_slots[n]) * irradiance
         else:
-            row_key = lax.broadcasted_iota(jnp.int32, (groups_dev * BD, count), 0) + z * (groups_dev * BD)
+            out_row = lax.broadcasted_iota(jnp.int32, (BD * groups_dev, count), 0)
+            row_key = (out_row % groups_dev + z * groups_dev) * BD + out_row // groups_dev
             select = jnp.where(row_key == key_row, jnp.ones(row_key.shape, F32), 0.0).astype(BF16)
             high = terms.astype(BF16)
             low = (terms - high.astype(F32)).astype(BF16)
             inc_all[...] = jnp.dot(select, high, preferred_element_type=F32) + jnp.dot(
                 select, low, preferred_element_type=F32
             )
-            for g in range(groups_dev):
-                emis = emis_cols[0]
-                for k in range(1, NCLS):
-                    emis = jnp.where(coat_ref[g] == k, emis_cols[k], emis)
-                piece = inc_all[g * BD : (g + 1) * BD, :]
-                received = emis * piece
-                inc_ref[g] = piece
-                sum_last[x, g : g + 1, :] = jnp.sum(received, axis=0, keepdims=True) / held[1, g : g + 1, :]
+            partial = jnp.zeros((groups_dev, FG), F32)
+            for b in range(BD):
+                irradiance = inc_all[b * groups_dev : (b + 1) * groups_dev, :] / held[1]
+                inc_all[b * groups_dev : (b + 1) * groups_dev, :] = irradiance
+                partial = partial + emis_held[b] * irradiance
+            sum_last[x] = partial
             band_copies.extend(over_band(sum_last, sum_send.at[1], sum_recv.at[1]))
             from_band(sum_last, sum_send.at[1], sum_recv.at[1])
             absorbed = sum_last[0]
             for xx in range(1, X):
                 absorbed = absorbed + sum_last[xx]
-            fourth_ref[...] = (absorbed + held[2]) / emit_held[...]
+            fourth = (absorbed + held[2]) / emit_held[...]
+            fourth_ref[...] = fourth
+            for b in range(BD):
+                irradiance = inc_all[b * groups_dev : (b + 1) * groups_dev, :]
+                result = weight_held[b] * fourth + (1.0 - emis_held[b]) * irradiance
+                out_ref[b] = result.astype(BF16)
         for copy in started:
             copy.wait_send()
     for copy in info_copies + row_copies + band_copies:
@@ -344,25 +361,18 @@
     NCLS, NB = emis_table.shape
     NM = share_table.shape[0]
     Z, X, C = lax.axis_size("grp"), lax.axis_size("band"), lax.axis_size("half")
-    x = lax.axis_index("band")
     pairs_dev = pair_list.shape[0]
     ppd = pairs_dev // X
     S = 2 * ppd
     D = Z * C
     bands_dev = NB // X
 
-    def emis_of(classes):
-        result = jnp.zeros((classes.shape[0], NB), F32)
-        for k in range(NCLS):
-            result = jnp.where((classes == k)[:, None], emis_table[k][None, :], result)
-        return result
-
     smem = pl.BlockSpec(memory_space=pltpu.SMEM)
     dma = pltpu.SemaphoreType.DMA
-    incoming, fourth = pl.pallas_call(
+    radiosity, fourth = pl.pallas_call(
         functools.partial(exchange, (Z, X, C, S, ppd, NB, NM, NCLS)),
         out_shape=(
-            jax.ShapeDtypeStruct((groups_dev, bands_dev, FG), F32),
+            jax.ShapeDtypeStruct((bands_dev, groups_dev, FG), BF16),
             jax.ShapeDtypeStruct((groups_dev, FG), F32),
         ),
         in_specs=[smem] * 4 + [pl.BlockSpec(memory_space=pl.ANY)] * 5,
@@ -384,6 +394,7 @@
             pltpu.VMEM((X, groups_dev, FG), F32),
             pltpu.VMEM((groups_dev, FG), F32),
             pltpu.VMEM((groups_dev * bands_dev, FG), F32),
+            pltpu.VMEM((bands_dev, groups_dev, FG), F32),
             dma((3,)),
             dma(()),
             dma(()),
@@ -407,20 +418,7 @@
         material, start_t4, facet_areas, heat_load, kernel,
     )
 
-    emis = emis_of(coating)[:, :, None]
-
-    def mine(rows):
-        return lax.dynamic_slice_in_dim(rows, x * bands_dev, bands_dev, 1)
-
-    share_mine = jnp.zeros((groups_dev, bands_dev, FG), F32)
-    table = mine(share_table)
-    for m in range(NM):
-        share_mine = jnp.where((material == m)[:, None, :], table[m][None, :, None], share_mine)
-    emis_mine = mine(emis)
-    radiosity = emis_mine * share_mine * fourth[:, None, :] + (1.0 - emis_mine) * (
-        incoming / facet_areas[:, None, :]
-    )
-    return (radiosity.astype(BF16), fourth**0.25)
+    return (radiosity.transpose(1, 0, 2), fourth**0.25)
 
 
 def solution(mesh):

time: 65.2 us -> 59.7 us (0.916)
  other arithmetic: 4.82 us -> 0 us
    convert_element_type x1 -> x0, other arithmetic: 3.02 us -> none  [on_device(): return (radiosity.astype(BF16), fourth ** 0.25)]
    unnamed x3 -> x2, local copies, waits for them, and re-layouts: 1.38 us -> 3.19 us
    eq x2 -> x0, other arithmetic: 1.72 us -> none  [the longest x1 1.06 us: on_device(): material == m]
    broadcast_in_dim x2 -> x0, local copies, waits for them, and re-layouts: 0.84 us -> none  [the longest x1 0.83 us: emis_of(): result = jnp.where((classes == k)[:, None], emis_table[k][None, :], result)]
    dynamic_slice x1 -> x0, local copies, waits for them, and re-layouts: 0.76 us -> none  [mine(): return lax.dynamic_slice_in_dim(rows, x * bands_dev, bands_dev, 1)]
where the time goes in v3:
time: 59.7 us; the launch traced here: 59.4 us
  Pallas kernels  54 us (90%)
  local copies, waits for them, and re-layouts  4.8 us (8%)
  between operations  0.64 us (1%)
    pallas_call x1, Pallas kernels, on_device(): pl.pallas_call(functools.partial(exchange, (Z, X, C, S, ppd, NB, NM, NCLS...  54 us
    unnamed x2, local copies, waits for them, and re-layouts  3.19 us
    pow x1, local copies, waits for them, and re-layouts, on_device(): return (radiosity.transpose(1, 0, 2), fourth ** 0.25)  1.61 us

profile of v3, /device:TPU:9, one launch (start us, length us, event | category | flops | bytes accessed | tf_op | source)
XLA Modules:
  0.0 59.4 jit_solution(12003178200474268409)
XLA Ops:
  0.6 1.3 %copy.11.refs_0_ = s32[4,2]{1,0:T(4,128)} copy(s32[4,2]{0,1:T(2,128)} %param.9) | data formatting | bytes 64 | tf_op args[0]
  2.0 54.0 %shard_map.104 = (bf16[4,32,1024]{2,1,0:T(8,128)(2,1)}, f32[32,1024]{1,0:T(8,128)}) custom-call(s32[4,2]{1,0:T(4,128)} %copy.11.refs_0_, s32[32]{0:T(128)} %refs_1_.1, f32[4,8]{1,0:T(4,128)} %refs_2_.1, f32[8,8]{1,0:T(8,128)} %refs_3_.1, s32[32,1024]{1,0:T(8,128)} %refs_4_.1, f32[32,1024]{1,0:T(8,128)} %refs_5_.1, f32[32,1024]{1,0:T(8,128)} %refs_6_.1, ...), custom_call_target="tpu_custom_call" | custom-call | flops 200000000 | bytes 8000000 | tf_op jit(solution)/shard_map/pallas_call | solution.py:372
  56.0 1.9 %copy.12 = bf16[32,4,1024]{2,1,0:T(4,128)(2,1)} copy(bf16[32,4,1024]{2,0,1:T(8,128)(2,1)} %bitcast.1) | data formatting | bytes 524288
  57.8 1.6 %broadcast_power_fusion = f32[32,1024]{1,0:T(8,128)} fusion(f32[32,1024]{1,0:T(8,128)} %get-tuple-element.5), kind=kLoop, calls=%fused_computation | loop fusion | bytes 262144 | tf_op jit(solution)/shard_map/pow | solution.py:421

commit v4 on v3

--- a/solution.py
+++ b/solution.py
@@ -418,7 +418,7 @@
         material, start_t4, facet_areas, heat_load, kernel,
     )
 
-    return (radiosity.transpose(1, 0, 2), fourth**0.25)
+    return (radiosity.transpose(1, 0, 2), jnp.sqrt(jnp.sqrt(fourth)))
 
 
 def solution(mesh):

time: 59.7 us -> 59.7 us (level)
    sqrt x0 -> x1, local copies, waits for them, and re-layouts: none -> 1.62 us  [on_device(): return (radiosity.transpose(1, 0, 2), jnp.sqrt(jnp.sqrt(fourth)))]
    pow x1 -> x0, local copies, waits for them, and re-layouts: 1.61 us -> none  [on_device(): return (radiosity.transpose(1, 0, 2), fourth ** 0.25)]
where the time goes in v4:
time: 59.7 us; the launch traced here: 59.5 us
  Pallas kernels  54 us (90%)
  local copies, waits for them, and re-layouts  4.82 us (8%)
  between operations  0.64 us (1%)
    pallas_call x1, Pallas kernels, on_device(): pl.pallas_call(functools.partial(exchange, (Z, X, C, S, ppd, NB, NM, NCLS...  54 us
    unnamed x2, local copies, waits for them, and re-layouts  3.19 us
    sqrt x1, local copies, waits for them, and re-layouts, on_device(): return (radiosity.transpose(1, 0, 2), jnp.sqrt(jnp.sqrt(fourth)))  1.62 us

profile of v4, /device:TPU:9, one launch (start us, length us, event | category | flops | bytes accessed | tf_op | source)
XLA Modules:
  0.0 59.5 jit_solution(2426588279912556947)
XLA Ops:
  0.6 1.3 %copy.11.refs_0_ = s32[4,2]{1,0:T(4,128)} copy(s32[4,2]{0,1:T(2,128)} %param.9) | data formatting | bytes 64 | tf_op args[0]
  2.0 54.0 %shard_map.104 = (bf16[4,32,1024]{2,1,0:T(8,128)(2,1)}, f32[32,1024]{1,0:T(8,128)}) custom-call(s32[4,2]{1,0:T(4,128)} %copy.11.refs_0_, s32[32]{0:T(128)} %refs_1_.1, f32[4,8]{1,0:T(4,128)} %refs_2_.1, f32[8,8]{1,0:T(8,128)} %refs_3_.1, s32[32,1024]{1,0:T(8,128)} %refs_4_.1, f32[32,1024]{1,0:T(8,128)} %refs_5_.1, f32[32,1024]{1,0:T(8,128)} %refs_6_.1, ...), custom_call_target="tpu_custom_call" | custom-call | flops 200000000 | bytes 8000000 | tf_op jit(solution)/shard_map/pallas_call | solution.py:372
  56.0 1.9 %copy.12 = bf16[32,4,1024]{2,1,0:T(4,128)(2,1)} copy(bf16[32,4,1024]{2,0,1:T(8,128)(2,1)} %bitcast.1) | data formatting | bytes 524288
  57.8 1.6 %sqrt_sqrt_fusion = f32[32,1024]{1,0:T(8,128)} fusion(f32[32,1024]{1,0:T(8,128)} %get-tuple-element.5), kind=kLoop, calls=%fused_computation | loop fusion | bytes 262144 | tf_op jit(solution)/shard_map/sqrt | solution.py:421
